TPU v7x, 32 devices: a whole 2x2x4 slice. The times are simulated.
32 devices in a mesh: group: 4 (over x, core), inner: 8 (over z, y).
Axes of the slice: x: 2, y: 2, z: 4, core: 2. Of those that a mesh axis runs over, the one named last changes fastest.
Arguments:
- x_self: bfloat16 [32768, 256], P(('group', 'inner')), may hold values from -6 to 6
- x_agg: bfloat16 [32768, 256], P(('group', 'inner')), may hold values from -6 to 6
- w_self: bfloat16 [256, 256], replicated, may hold values from -0.25 to 0.25
- w_nbr: bfloat16 [256, 256], replicated, may hold values from -0.25 to 0.25
- b_layer: float32 [256], replicated, may hold values from -3 to 3
- w_one: bfloat16 [256, 512], replicated, may hold values from -0.375 to 0.375
- b_one: float32 [512], replicated, may hold values from -3 to 3
- w_two: bfloat16 [512, 512], replicated, may hold values from -0.25 to 0.25
- b_two: float32 [512], replicated, may hold values from -3 to 3
- w_out: float32 [512], replicated, may hold values from -2 to 2
- send_lists: int32 [128, 8, 96], P(('group', 'inner')), may hold values from 0 to 1023, as said below
- endpoint_slots: int32 [16384, 2], P(('group', 'inner')), may hold values from 0 to 3071, as said below
- neg_index: int32 [16384, 4], P(('group', 'inner')), may hold values from 0 to 511, as said below
Outputs:
- grad_self: bfloat16 [32768, 256], P(('group', 'inner'))
- grad_agg: bfloat16 [32768, 256], P(('group', 'inner'))
- grad_scorer: float32 [393216], P(('group', 'inner'))
- grad_layer: float32 [131072], P(('group', 'inner'))
- grad_bias: float32 [1792], replicated
Inputs may be any that keep to these rules, and one draw needn't show every extreme that they name: `send_lists`: viewed as [32, 32, 96] (owner, requesting device, slot), each entry is a row of the owner's block of 1024 nodes, and the 96 entries of one owner and one requesting device are distinct. Slots that endpoint_slots never names hold arbitrary rows. `endpoint_slots`: each entry of device r's block is a slot o * 96 + c of that device and names the node of send_lists' entry (o, r, c). `neg_index`: entry [p, k] is the index, within the same block of 512 positives, of another positive whose destination serves as the k-th negative of p; it is never p itself.
All inputs are finite; a program needn't handle non-finite values.
Results may differ from a plain program's by a relative error of at most 0.0075.
Values may be sent and summed in bfloat16 or wider, within the bound.
A program may use at most 128 MiB of HBM per device.

v0:
```python
import functools

import jax
import jax.numpy as jnp
from jax import lax
from jax.experimental import pallas as pl
from jax.experimental.pallas import tpu as pltpu
from jax.sharding import PartitionSpec as P

MESH = pl.DeviceIdType.MESH
VMEM = pltpu.VMEM
LOW = jnp.bfloat16


def silu_slope(inputs):
    sigmoid_of = jax.nn.sigmoid(inputs)
    return sigmoid_of * (1.0 + inputs * (1.0 - sigmoid_of))


def dot_first(first_op, second_op):
    return lax.dot_general(
        first_op, second_op, (((0,), (0,)), ((), ())), preferred_element_type=jnp.float32
    )


def dot_last(first_op, second_op):
    return lax.dot_general(
        first_op, second_op, (((1,), (1,)), ((), ())), preferred_element_type=jnp.float32
    )


def dot_plain(first_op, second_op):
    return jnp.dot(first_op, second_op, preferred_element_type=jnp.float32)


def place(groups, inners):
    group = lax.axis_index("group")
    inner = lax.axis_index("inner")
    return group, inner, group * inners + inner


def peer_of(groups, inners, step):
    group, inner, _ = place(groups, inners)
    middle = inners // 2
    turn = step - 1
    turn = turn + jnp.where(turn >= (inners - middle) * groups, 1, 0)
    to_inner = lax.rem(inner + middle + turn // groups, inners)
    return lax.rem(group + lax.rem(turn, groups), groups) * inners + to_inner


def greet_all(groups, inners):
    barrier = pltpu.get_barrier_semaphore()

    def greet(step, carry):
        peer = peer_of(groups, inners, step)
        pl.semaphore_signal(
            barrier,
            inc=1,
            device_id=(peer // inners, lax.rem(peer, inners)),
            device_id_type=MESH,
        )
        return carry

    lax.fori_loop(1, groups * inners, greet, 0)


def exchange_copy(groups, inners, step, landing, src, dst, sends, recvs):
    _, _, me = place(groups, inners)
    peer = peer_of(groups, inners, step)
    slot = peer if landing else me
    return pltpu.make_async_remote_copy(
        src_ref=src.at[peer],
        dst_ref=dst.at[slot],
        send_sem=sends.at[peer],
        recv_sem=recvs.at[slot],
        device_id=(peer // inners, lax.rem(peer, inners)),
        device_id_type=MESH,
    )


def exchange(groups, inners, make, src, dst, sends, recvs):
    def start(step, carry):
        peer = peer_of(groups, inners, step)
        src[peer] = make(peer)
        exchange_copy(groups, inners, step, False, src, dst, sends, recvs).start()
        return carry

    lax.fori_loop(1, groups * inners, start, 0)
    _, _, me = place(groups, inners)
    dst[me] = make(me)


def exchange_wait(groups, inners, src, dst, sends, recvs):
    def finish(step, carry):
        copy = exchange_copy(groups, inners, step, True, src, dst, sends, recvs)
        copy.wait_send()
        copy.wait_recv()
        return carry

    lax.fori_loop(1, groups * inners, finish, 0)


def axis_copy(groups, inners, along, step, landing, src, dst, sends, recvs, whole):
    group, inner, _ = place(groups, inners)
    if along == "group":
        mine, peer = group, lax.rem(group + step, groups)
        device = (peer, inner)
    else:
        mine, peer = inner, lax.rem(inner + step, inners)
        device = (group, peer)
    slot = peer if landing else mine
    return pltpu.make_async_remote_copy(
        src_ref=src if whole else src.at[peer],
        dst_ref=dst.at[slot],
        send_sem=sends.at[peer],
        recv_sem=recvs.at[slot],
        device_id=device,
        device_id_type=MESH,
    )


def axis_start(groups, inners, along, src, dst, sends, recvs, whole=False):
    for step in range(1, groups if along == "group" else inners):
        axis_copy(
            groups, inners, along, step, False, src, dst, sends, recvs, whole
        ).start()


def axis_wait(groups, inners, along, src, dst, sends, recvs, whole=False):
    for step in range(1, groups if along == "group" else inners):
        copy = axis_copy(groups, inners, along, step, True, src, dst, sends, recvs, whole)
        copy.wait_send()
        copy.wait_recv()


def share_middle(groups, inners, halves, src, land_one, stage, land_two):
    group, inner, _ = place(groups, inners)
    land_one[group] = src[group]
    total = land_one[0].astype(jnp.float32)
    for index in range(1, groups):
        total = total + land_one[index].astype(jnp.float32)
    rows, width = total.shape[0] // inners, total.shape[1]
    half = width // halves
    for index in range(inners):
        part = total[index * rows : (index + 1) * rows]
        if halves > 1:
            part = jnp.concatenate(
                [part[:, side * half : (side + 1) * half] for side in range(halves)], axis=0
            )
        stage[index, : rows * halves] = part.astype(stage.dtype)
    land_two[inner] = stage[inner]


def sum_slots(count, landed):
    total = landed[0].astype(jnp.float32)
    for index in range(1, count):
        total = total + landed[index].astype(jnp.float32)
    return total


def hot(mask):
    return jnp.where(mask, 1.0, 0.0).astype(LOW)


def iota(rows, columns, dim):
    return lax.broadcasted_iota(jnp.int32, (rows, columns), dim)


def sigmoid(values):
    return 0.5 * jnp.tanh(0.5 * values) + 0.5


def kernel(
    groups,
    inners,
    block,
    x_self,
    x_agg,
    w_self,
    w_nbr,
    b_layer,
    w_one,
    b_one,
    w_two,
    b_two,
    w_out,
    lists,
    ends_pair,
    negs,
    d_pre_low,
    scorer_share,
    layer_share,
    bias_out,
    pre_act,
    table,
    outgoing,
    fetched,
    outbound,
    received,
    end_rows,
    end_grads,
    end_low,
    joint,
    h_one,
    d_two_low,
    d_one_low,
    weight_sum,
    hidden_sums,
    layer_sum,
    terms_a,
    land_a,
    stage_a,
    final_a,
    terms_b,
    land_b,
    stage_b,
    final_b,
    bias,
    bias_land,
    bias_stage,
    bias_final,
    lists_wide,
    lists_tall,
    lists_row,
    index_wide,
    index_tall,
    ends_row,
    f_sends,
    f_recvs,
    r_sends,
    r_recvs,
    ag_sends,
    ag_recvs,
    ai_sends,
    ai_recvs,
    bg_sends,
    bg_recvs,
    bi_sends,
    bi_recvs,
    cg_sends,
    cg_recvs,
    ci_sends,
    ci_recvs,
):
    owners = groups * inners
    group, inner, me = place(groups, inners)
    nodes, width = x_self.shape
    padded = outgoing.shape[1]
    slots = owners * padded
    ends = end_rows.shape[0]
    pos = ends // 2
    halves = pos // block
    blocks = joint.shape[0]
    pairs = blocks * block
    hidden = w_two.shape[0]

    greet_all(groups, inners)
    lists_wide[...] = jnp.zeros_like(lists_wide)
    lists_wide[:owners, :padded] = lists[...].astype(jnp.float32)
    lists_tall[...] = jnp.transpose(lists_wide[...])

    def column(values, index):
        chosen = jnp.where(iota(*values.shape, 1) == index, values, 0.0)
        return jnp.sum(chosen, axis=1, keepdims=True).astype(jnp.int32)

    def node_step(step, carry):
        rows = pl.ds(pl.multiple_of(step * block, block), block)
        acts = dot_plain(x_self[rows], w_self[...]) + dot_plain(x_agg[rows], w_nbr[...])
        acts = acts + b_layer[...]
        pre_act[rows] = acts
        table[rows] = (acts * sigmoid(acts)).astype(LOW)
        return carry

    lax.fori_loop(0, nodes // block, node_step, 0)
    pl.semaphore_wait(pltpu.get_barrier_semaphore(), owners - 1)

    def make_rows(peer):
        chosen = hot(column(lists_tall[:padded], peer) == iota(padded, nodes, 1))
        return dot_plain(chosen, table[...]).astype(LOW)

    exchange(groups, inners, make_rows, outgoing, fetched, f_sends, f_recvs)


    index_wide[...] = jnp.zeros_like(index_wide)
    index_wide[:2] = ends_pair[...].astype(jnp.float32)
    index_wide[2 : 2 + negs.shape[0]] = negs[...].astype(jnp.float32)
    index_tall[...] = jnp.transpose(index_wide[...])
    for side in range(2):
        ends_row[:, side * pos : (side + 1) * pos] = ends_pair[side : side + 1]
    for owner in range(owners):
        lists_row[:, owner * padded : (owner + 1) * padded] = lists[owner : owner + 1]
    end_grads[...] = jnp.zeros_like(end_grads)
    hidden_sums[...] = jnp.zeros_like(hidden_sums)
    weight_sum[...] = jnp.zeros_like(weight_sum)
    exchange_wait(groups, inners, outgoing, fetched, f_sends, f_recvs)

    def end_step(step, carry):
        rows = pl.ds(pl.multiple_of(step * block, block), block)
        part = pl.ds(pl.multiple_of(lax.rem(step, halves) * block, block), block)
        chosen = hot(column(index_tall[part], step // halves) == iota(block, slots, 1))
        all_rows = fetched[...].reshape(slots, width)
        end_rows[rows] = dot_plain(chosen, all_rows).astype(LOW)
        return carry

    lax.fori_loop(0, ends // block, end_step, 0)

    def pair_step(step, first):
        part = step if first else lax.rem(step, halves)
        rows = pl.ds(pl.multiple_of(part * block, block), block)
        dst_rows = pl.ds(pl.multiple_of(pos + part * block, block), block)
        left = end_rows[rows]
        if first:
            right = end_rows[dst_rows]
        else:
            chosen = hot(column(index_tall[rows], 1 + step // halves) == iota(block, pos, 1))
            right = dot_plain(chosen, end_rows[pos:]).astype(LOW)
        left = left.astype(jnp.float32)
        right = right.astype(jnp.float32)
        product = (left * right).astype(LOW)
        joint[step] = product
        a_one = dot_plain(product, w_one[...]) + b_one[...]
        s_one = sigmoid(a_one)
        slope_one = s_one * (1.0 + a_one * (1.0 - s_one))
        low_h = (a_one * s_one).astype(LOW)
        h_one[step] = low_h
        a_two = dot_plain(low_h, w_two[...]) + b_two[...]
        s_two = sigmoid(a_two)
        h_two = a_two * s_two
        scores = jnp.sum(h_two * w_out[...], axis=1, keepdims=True)
        slope = sigmoid(scores) - (1.0 if first else 0.0)
        d_two = slope * w_out[...] * (s_two * (1.0 + a_two * (1.0 - s_two)))
        low_two = d_two.astype(LOW)
        d_two_low[step] = low_two
        d_one = dot_last(low_two, w_two[...]) * slope_one
        low_one = d_one.astype(LOW)
        d_one_low[step] = low_one
        hidden_sums[0:1] += jnp.sum(d_one, axis=0, keepdims=True)
        hidden_sums[1:2] += jnp.sum(d_two, axis=0, keepdims=True)
        hidden_sums[2:3] += jnp.sum(slope * h_two, axis=0, keepdims=True)
        d_joint = dot_last(low_one, w_one[...])
        end_grads[rows] += d_joint * right
        d_right = d_joint * left
        if first:
            end_grads[dst_rows] += d_right
        else:
            along = negs[pl.ds(step // halves - 1, 1), rows]
            back = hot(iota(pos, block, 0) == along)
            end_grads[pos:] += dot_plain(back, d_right.astype(LOW))

    for step in range(halves):
        pair_step(step, True)

    def negative_step(step, carry):
        pair_step(step, False)
        return carry

    lax.fori_loop(halves, blocks, negative_step, 0)
    end_low[...] = end_grads[...].astype(LOW)

    def make_grads(peer):
        chosen = hot(iota(padded, ends, 0) + peer * padded == ends_row[...])
        return dot_plain(chosen, end_low[...]).astype(LOW)

    exchange(groups, inners, make_grads, outbound, received, r_sends, r_recvs)

    def weight_step(step, carry):
        weight_sum[:width] += dot_first(joint[step], d_one_low[step])
        weight_sum[width:] += dot_first(h_one[step], d_two_low[step])
        return carry

    lax.fori_loop(0, blocks, weight_step, 0)
    chunk = weight_sum.shape[0] // groups
    for index in range(groups):
        part = weight_sum[index * chunk : (index + 1) * chunk]
        terms_a[index] = (part / pairs).astype(LOW)
    axis_start(groups, inners, "group", terms_a, land_a, ag_sends, ag_recvs)
    axis_wait(groups, inners, "group", terms_a, land_a, ag_sends, ag_recvs)
    share_middle(groups, inners, 2, terms_a, land_a, stage_a, final_a)
    axis_start(groups, inners, "inner", stage_a, final_a, ai_sends, ai_recvs)
    exchange_wait(groups, inners, outbound, received, r_sends, r_recvs)

    layer_sum[...] = jnp.zeros_like(layer_sum)
    hidden_sums[3:4] = jnp.zeros((1, hidden), jnp.float32)

    def layer_step(step, carry):
        rows = pl.ds(pl.multiple_of(step * block, block), block)
        chosen = hot(iota(block, slots, 0) + step * block == lists_row[...])
        sums = dot_plain(chosen, received[...].reshape(slots, width))
        acts = pre_act[rows]
        s_act = sigmoid(acts)
        d_pre = sums * (s_act * (1.0 + acts * (1.0 - s_act)))
        low = d_pre.astype(LOW)
        d_pre_low[rows] = low
        hidden_sums[3:4, :width] += jnp.sum(d_pre, axis=0, keepdims=True)
        layer_sum[:width] += dot_first(x_self[rows], low)
        layer_sum[width:] += dot_first(x_agg[rows], low)
        return carry

    lax.fori_loop(0, nodes // block, layer_step, 0)
    layer_chunk = layer_sum.shape[0] // groups
    for index in range(groups):
        part = layer_sum[index * layer_chunk : (index + 1) * layer_chunk]
        terms_b[index] = (part / pairs).astype(LOW)
    bias[...] = jnp.zeros_like(bias)
    line = 0
    for row, span in ((0, hidden), (1, hidden), (2, hidden), (3, width)):
        for piece in range(span // 128):
            values = hidden_sums[row : row + 1, piece * 128 : (piece + 1) * 128]
            bias[line : line + 1] = values / pairs
            line += 1
    axis_start(groups, inners, "group", terms_b, land_b, bg_sends, bg_recvs)
    axis_start(groups, inners, "group", bias, bias_land, cg_sends, cg_recvs, True)
    axis_wait(groups, inners, "group", terms_b, land_b, bg_sends, bg_recvs)
    share_middle(groups, inners, 1, terms_b, land_b, stage_b, final_b)
    axis_start(groups, inners, "inner", stage_b, final_b, bi_sends, bi_recvs)
    axis_wait(groups, inners, "group", bias, bias_land, cg_sends, cg_recvs, True)
    bias_land[group] = bias[...]
    bias_stage[...] = sum_slots(groups, bias_land)
    bias_final[inner] = bias_stage[...]
    axis_start(groups, inners, "inner", bias_stage, bias_final, ci_sends, ci_recvs, True)
    axis_wait(groups, inners, "inner", stage_a, final_a, ai_sends, ai_recvs)
    total = sum_slots(inners, final_a)
    rows = chunk // inners
    half = hidden // 2
    scorer_share[:, :half] = total[:rows]
    scorer_share[:, half:] = total[rows : 2 * rows]
    axis_wait(groups, inners, "inner", stage_b, final_b, bi_sends, bi_recvs)
    layer_share[...] = sum_slots(inners, final_b)[: layer_chunk // inners]
    axis_wait(groups, inners, "inner", bias_stage, bias_final, ci_sends, ci_recvs, True)
    bias_out[...] = sum_slots(inners, bias_final)


def end_kernel(
    d_pre_low,
    w_self,
    w_nbr,
    scorer_share,
    layer_share,
    bias,
    grad_self,
    grad_agg,
    scorer_flat,
    layer_flat,
    bias_flat,
):
    grad_self[...] = dot_last(d_pre_low[...], w_self[...]).astype(LOW)
    grad_agg[...] = dot_last(d_pre_low[...], w_nbr[...]).astype(LOW)
    for share, flat in ((scorer_share, scorer_flat), (layer_share, layer_flat)):
        rows, width = share.shape
        lines = width // 128
        for line in range(lines):
            flat[pl.ds(line, rows, stride=lines)] = share[:, line * 128 : (line + 1) * 128]
    for line in range(bias_flat.shape[0] // 128):
        bias_flat[line * 128 : (line + 1) * 128] = bias[line]


def up_to(count, step):
    return -(-count // step) * step


def body(
    x_self,
    x_agg,
    w_self,
    w_nbr,
    b_layer,
    w_one,
    b_one,
    w_two,
    b_two,
    w_out,
    send_lists,
    endpoint_slots,
    neg_index,
):
    groups = lax.axis_size("group")
    inners = lax.axis_size("inner")
    owners = groups * inners
    nodes, width = x_self.shape
    hidden = w_two.shape[0]
    pos = endpoint_slots.shape[0]
    negatives = neg_index.shape[1]
    capacity = send_lists.shape[2]
    padded = up_to(capacity, 16)
    slots = owners * padded
    block = min(512, pos)
    blocks = pos * (1 + negatives) // block
    lists = send_lists.reshape(owners, capacity)
    ends = endpoint_slots.T
    negs = neg_index.T
    if padded != capacity:
        lists = jnp.pad(lists, ((0, 0), (0, padded - capacity)), constant_values=-1)
        ends = ends + (ends // capacity) * (padded - capacity)

    def f32(*shape):
        return VMEM(shape, jnp.float32)

    def low(*shape):
        return VMEM(shape, LOW)

    chunk_a = (width + hidden) // groups
    chunk_b = 2 * width // groups
    slab_a = up_to(2 * chunk_a // inners, 16)
    slab_b = up_to(chunk_b // inners, 16)
    lines = up_to((3 * hidden + width) // 128, 8)
    scratch = [
        f32(nodes, width),
        low(nodes, width),
        low(owners, padded, width),
        low(owners, padded, width),
        low(owners, padded, width),
        low(owners, padded, width),
        low(2 * pos, width),
        f32(2 * pos, width),
        low(2 * pos, width),
        low(blocks, block, width),
        low(blocks, block, hidden),
        low(blocks, block, hidden),
        low(blocks, block, hidden),
        f32(width + hidden, hidden),
        f32(8, hidden),
        f32(2 * width, width),
        low(groups, chunk_a, hidden),
        low(groups, chunk_a, hidden),
        low(inners, slab_a, hidden // 2),
        low(inners, slab_a, hidden // 2),
        low(groups, chunk_b, width),
        low(groups, chunk_b, width),
        low(inners, slab_b, width),
        low(inners, slab_b, width),
        f32(lines, 128),
        f32(groups, lines, 128),
        f32(lines, 128),
        f32(inners, lines, 128),
        f32(up_to(owners, 128), up_to(padded, 128)),
        f32(up_to(padded, 128), up_to(owners, 128)),
        VMEM((1, slots), jnp.int32),
        f32(128, pos),
        f32(pos, 128),
        VMEM((1, 2 * pos), jnp.int32),
    ]
    counts = [owners] * 4 + ([groups] * 2 + [inners] * 2) * 3
    flops = 2 * (pos * (1 + negatives) * 3 * hidden * (width + hidden))
    d_pre_low, scorer_share, layer_share, total = pl.pallas_call(
        functools.partial(kernel, groups, inners, block),
        out_shape=(
            jax.ShapeDtypeStruct((nodes, width), LOW),
            jax.ShapeDtypeStruct((chunk_a // inners, hidden), jnp.float32),
            jax.ShapeDtypeStruct((chunk_b // inners, width), jnp.float32),
            jax.ShapeDtypeStruct((lines, 128), jnp.float32),
        ),
        in_specs=[pl.BlockSpec(memory_space=VMEM)] * 13,
        out_specs=(pl.BlockSpec(memory_space=VMEM),) * 4,
        scratch_shapes=scratch + [pltpu.SemaphoreType.DMA((count,)) for count in counts],
        compiler_params=pltpu.CompilerParams(
            collective_id=0, has_side_effects=True, vmem_limit_bytes=56 * 1024 * 1024
        ),
        cost_estimate=pl.CostEstimate(flops=flops, bytes_accessed=2**23, transcendentals=2**22),
        name="link_backward",
    )(
        x_self,
        x_agg,
        w_self,
        w_nbr,
        b_layer[None],
        w_one,
        b_one[None],
        w_two,
        b_two[None],
        w_out[None],
        lists,
        ends,
        negs,
    )
    share_a, share_b = scorer_share.size, layer_share.size
    grad_self, grad_agg, scorer_flat, layer_flat, bias_total = pl.pallas_call(
        end_kernel,
        out_shape=(
            jax.ShapeDtypeStruct((nodes, width), LOW),
            jax.ShapeDtypeStruct((nodes, width), LOW),
            jax.ShapeDtypeStruct((share_a // 128, 128), jnp.float32),
            jax.ShapeDtypeStruct((share_b // 128, 128), jnp.float32),
            jax.ShapeDtypeStruct((3 * hidden + width,), jnp.float32),
        ),
        in_specs=[pl.BlockSpec(memory_space=VMEM)] * 6,
        out_specs=(pl.BlockSpec(memory_space=VMEM),) * 5,
        compiler_params=pltpu.CompilerParams(vmem_limit_bytes=32 * 1024 * 1024),
        name="end_products",
    )(d_pre_low, w_self, w_nbr, scorer_share, layer_share, total)
    return (grad_self, grad_agg, scorer_flat.reshape(-1), layer_flat.reshape(-1), bias_total)


def solution(mesh):
    rows = P(("group", "inner"), None)
    flat = P(("group", "inner"))
    return jax.shard_map(
        body,
        mesh=mesh,
        in_specs=(rows, rows) + (P(),) * 8 + (P(("group", "inner"), None, None), rows, rows),
        out_specs=(rows, rows, flat, flat, P()),
        check_vma=False,
    )
```

profile of v0, /device:TPU:0, one launch (start us, length us, event | category | flops | bytes accessed | tf_op | source)
XLA Modules:
  0.0 115.5 jit_solution(7990023469180280644)
XLA Ops:
  0.6 0.0 copy-start.1
  0.6 0.0 copy-start.2
  0.7 110.1 %link_backward.1 = (bf16[1024,256]{1,0:T(8,128)(2,1)}, f32[24,512]{1,0:T(8,128)}, f32[16,256]{1,0:T(8,128)}, f32[16,128]{1,0:T(8,128)}) custom-call(bf16[1024,256]{1,0:T(8,128)(2,1)} %x_self.1, bf16[1024,256]{1,0:T(8,128)(2,1)} %x_agg.1, bf16[256,256]{1,0:T(8,128)(2,1)} %w_self.3, bf16[256,256]{1,0:T(8,128)(2,1)} %w_nbr.3, f32[1,256]{1,0:T(1,128)} %bitcast.17, ...), custom_call_target="tpu_custom_call" | custom-call | flops 6039797760 | bytes 8388608 | tf_op jit(solution)/shard_map/link_backward/pallas_call | solution.py:544
  110.8 0.0 copy-done.1
  110.8 0.0 copy-done.2
  110.8 0.0 copy-start
  110.8 1.0 copy-done
  111.8 0.0 copy-start.3
  111.8 0.8 copy-done.3
  112.6 0.0 copy-start.4
  112.6 0.7 copy-done.4
  113.3 0.0 copy-start.5
  113.3 0.7 copy-done.5
  114.0 1.4 %end_products.1 = (bf16[1024,256]{1,0:T(8,128)(2,1)}, bf16[1024,256]{1,0:T(8,128)(2,1)}, f32[96,128]{1,0:T(8,128)}, f32[32,128]{1,0:T(8,128)}, f32[1792]{0:T(1024)}) custom-call(bf16[1024,256]{1,0:T(8,128)(2,1)S(1)} %copy-done, bf16[256,256]{1,0:T(8,128)(2,1)S(1)} %copy-done.1, bf16[256,256]{1,0:T(8,128)(2,1)S(1)} %copy-done.2, f32[24,512]{1,0:T(8,128)S(1)} %copy-done.3, ...), custom_call_target="tpu_custom_call" | custom-call | tf_op jit(solution)/shard_map/end_products/pallas_call | solution.py:576
Async XLA Ops:
  0.6 110.1 %copy-start.1 = (bf16[256,256]{1,0:T(8,128)(2,1)S(1)}, bf16[256,256]{1,0:T(8,128)(2,1)}, u32[]{:S(2)}) copy-start(bf16[256,256]{1,0:T(8,128)(2,1)} %w_self.3) | copy-start | bytes 393220
  0.6 110.1 %copy-start.2 = (bf16[256,256]{1,0:T(8,128)(2,1)S(1)}, bf16[256,256]{1,0:T(8,128)(2,1)}, u32[]{:S(2)}) copy-start(bf16[256,256]{1,0:T(8,128)(2,1)} %w_nbr.3) | copy-start | bytes 393220
  110.8 1.0 copy-start
  111.8 0.8 copy-start.3
  112.6 0.7 copy-start.4
  113.3 0.7 copy-start.5
where the time goes:
time: 116 us; the launch traced here: 115 us
  Pallas kernels  112 us (97%)
  local copies, waits for them, and re-layouts  3.25 us (3%)
    pallas_call x1, Pallas kernels, body(): pl.pallas_call(functools.partial(kernel, groups, inners, block), out_shap...  110 us
    unnamed x12, local copies, waits for them, and re-layouts  3.25 us

commit v1 on v0

--- a/solution.py
+++ b/solution.py
@@ -584,7 +584,7 @@
         ),
         in_specs=[pl.BlockSpec(memory_space=VMEM)] * 6,
         out_specs=(pl.BlockSpec(memory_space=VMEM),) * 5,
-        compiler_params=pltpu.CompilerParams(vmem_limit_bytes=32 * 1024 * 1024),
+        compiler_params=pltpu.CompilerParams(vmem_limit_bytes=60 * 1024 * 1024),
         name="end_products",
     )(d_pre_low, w_self, w_nbr, scorer_share, layer_share, total)
     return (grad_self, grad_agg, scorer_flat.reshape(-1), layer_flat.reshape(-1), bias_total)

time: 116 us -> 113 us (0.974)
  local copies, waits for them, and re-layouts: 3.25 us -> 0 us
    unnamed x12 -> x0, local copies, waits for them, and re-layouts: 3.25 us -> none
    pallas_call x1, Pallas kernels: 1.43 us -> 2.61 us  [body(): pl.pallas_call(end_kernel, out_shape=(jax.ShapeDtypeStruct((nodes, width)...]
where the time goes in v1:
time: 113 us
  Pallas kernels  113 us (100%)
    pallas_call x1, Pallas kernels, body(): pl.pallas_call(functools.partial(kernel, groups, inners, block), out_shap...  110 us
    pallas_call x1, Pallas kernels, body(): pl.pallas_call(end_kernel, out_shape=(jax.ShapeDtypeStruct((nodes, width)...  2.61 us

profile of v1, /device:TPU:0, one launch (start us, length us, event | category | flops | bytes accessed | tf_op | source)
XLA Modules:
  0.0 113.3 jit_solution(8380013508147353508)
XLA Ops:
  0.6 110.0 %link_backward.1 = (bf16[1024,256]{1,0:T(8,128)(2,1)}, f32[24,512]{1,0:T(8,128)}, f32[16,256]{1,0:T(8,128)}, f32[16,128]{1,0:T(8,128)}) custom-call(bf16[1024,256]{1,0:T(8,128)(2,1)} %x_self.1, bf16[1024,256]{1,0:T(8,128)(2,1)} %x_agg.1, bf16[256,256]{1,0:T(8,128)(2,1)} %w_self.3, bf16[256,256]{1,0:T(8,128)(2,1)} %w_nbr.3, f32[1,256]{1,0:T(1,128)} %bitcast.17, ...), custom_call_target="tpu_custom_call" | custom-call | flops 6039797760 | bytes 8388608 | tf_op jit(solution)/shard_map/link_backward/pallas_call | solution.py:544
  110.7 2.6 %end_products.1 = (bf16[1024,256]{1,0:T(8,128)(2,1)}, bf16[1024,256]{1,0:T(8,128)(2,1)}, f32[96,128]{1,0:T(8,128)}, f32[32,128]{1,0:T(8,128)}, f32[1792]{0:T(1024)}) custom-call(bf16[1024,256]{1,0:T(8,128)(2,1)} %get-tuple-element.14.d_pre_low, bf16[256,256]{1,0:T(8,128)(2,1)} %w_self.3, bf16[256,256]{1,0:T(8,128)(2,1)} %w_nbr.3, ...), custom_call_target="tpu_custom_call" | custom-call | tf_op jit(solution)/shard_map/end_products/pallas_call | solution.py:576
